TPU v7x, 32 devices: a whole 2x2x4 slice. The times are simulated.
32 devices in a mesh: segment: 4 (over y, x), dp: 8 (over z, core).
Axes of the slice: x: 2, y: 2, z: 4, core: 2. Of those that a mesh axis runs over, the one named last changes fastest.
Arguments:
- x_saved: bfloat16 [4, 1024, 1536], P('segment', 'dp'), may hold values from -6 to 6
- gains: float32 [4, 1536], P('segment'), may hold values from 0.1 to 1.9
- w_in: bfloat16 [4, 1536, 3072], P('segment', 'dp'), may hold values from -0.15625 to 0.15625
- w_out: bfloat16 [4, 3072, 1536], P('segment', None, 'dp'), may hold values from -0.109375 to 0.109375
- cotangent: bfloat16 [1024, 1536], P('dp'), may hold values from -6 to 6
- lengths: int32 [8], replicated, may hold values from 1 to 256, 1024 in all
Outputs:
- grads: bfloat16 [4, 1024, 1536], P('segment', 'dp')
- gain_grads: float32 [4, 1536], P('segment')
All inputs are finite; a program needn't handle non-finite values.
Results may differ from a plain program's by a relative error of at most 0.0075.
Values may be sent and summed in bfloat16 or wider, within the bound.
A program may use at most 128 MiB of HBM per device.

v0:
```python
import jax
import jax.numpy as jnp
from jax import lax
from jax.sharding import PartitionSpec as P


def passed_along(x, axis, by):
    length = lax.axis_size(axis)
    pairs = [(i, i + by) for i in range(length) if 0 <= i + by < length]
    return lax.ppermute(x, axis, pairs)


def on_device(x_saved, gains, w_in, w_out, cotangent, lengths):
    rows = cotangent.shape[0]
    width = cotangent.shape[1]
    ends = jnp.cumsum(lengths)
    position = lax.axis_index("dp") * rows + jnp.arange(rows, dtype=jnp.int32)
    utter_hit = (position[:, None] >= ends[None, :]).astype(jnp.int32)
    utter = jnp.sum(utter_hit, 1)
    onehot = (utter[:, None] == jnp.arange(lengths.shape[0], dtype=jnp.int32)[None, :]).astype(
        jnp.int32
    )
    tok_len = jnp.sum(onehot * lengths[None, :], 1).astype(jnp.float32)
    weight = 2.0 * rows / (tok_len + rows)
    current = (cotangent.astype(jnp.float32) * weight[:, None]).astype(jnp.bfloat16)
    xf = x_saved[0].astype(jnp.float32)
    centered_input = xf - jnp.mean(xf, -1, keepdims=True)
    variance = jnp.mean(centered_input * centered_input, -1, keepdims=True)
    inverse_deviation = lax.rsqrt(variance + 1e-05)
    standardized_input = centered_input * inverse_deviation
    gain_vector = gains[0]
    normalized_input = (standardized_input * gain_vector).astype(jnp.bfloat16)
    w_first, w_second = (
        lax.all_gather(w_in[0], "dp", axis=0, tiled=True),
        lax.all_gather(w_out[0], "dp", axis=1, tiled=True),
    )

    def project_all(normed_rows, grad_in):
        hidden = jnp.dot(normed_rows, w_first, preferred_element_type=jnp.float32)
        up_grad = jnp.dot(grad_in, w_second.T, preferred_element_type=jnp.float32)
        sig = jax.nn.sigmoid(hidden)
        hid_grad = (0.5 * up_grad * (sig + hidden * sig * (1.0 - sig))).astype(jnp.bfloat16)
        return jnp.dot(hid_grad, w_first.T, preferred_element_type=jnp.float32)

    def block_back():

        def run(grad_in):
            norm_gradient = project_all(normalized_input, grad_in)
            gain_partial = jnp.sum(norm_gradient * standardized_input, 0)
            gain_scaled = norm_gradient * gain_vector
            backward_result = inverse_deviation * (
                gain_scaled
                - jnp.mean(gain_scaled, -1, keepdims=True)
                - standardized_input * jnp.mean(gain_scaled * standardized_input, -1, keepdims=True)
            )
            return (
                (grad_in.astype(jnp.float32) + backward_result).astype(jnp.bfloat16),
                gain_partial,
            )

        return run

    def pass_through(grad_in):
        return (grad_in, jnp.zeros((width,), jnp.float32))

    segments = lax.axis_size("segment")
    my_segment = lax.axis_index("segment")
    gain_local = jnp.zeros((width,), jnp.float32)
    result = current
    for level in range(segments - 1, -1, -1):
        mine = my_segment == level
        updated, gain_partial = lax.cond(mine, block_back(), pass_through, current)
        result = jnp.where(mine, updated, result)
        gain_local = jnp.where(mine, gain_partial, gain_local)
        if level > 0:
            current = passed_along(updated, "segment", -1)
    gain_total = lax.psum(gain_local, "dp")
    return (result[None], gain_total[None])


def solution(mesh):
    in_specs = (
        P("segment", "dp", None),
        P("segment", None),
        P("segment", "dp", None),
        P("segment", None, "dp"),
        P("dp", None),
        P(),
    )
    out_specs = (P("segment", "dp", None), P("segment", None))
    return jax.shard_map(
        on_device, mesh=mesh, in_specs=in_specs, out_specs=out_specs, check_vma=False
    )
```

profile of v0, /device:TPU:0, one launch (start us, length us, event | category | flops | bytes accessed | tf_op | source)
XLA Modules:
  0.0 331.9 jit_solution(3491810333015063255)
XLA Ops:
  7.2 0.0 copy-start.10
  7.2 0.0 copy-start.2
  7.2 0.0 copy-start
  7.2 0.0 copy-start.1
  7.2 0.0 all-gather.7.cloned.1.call-start
  7.2 0.7 all-gather.7.cloned.1.call-update
  7.9 0.0 all-gather.5.cloned.1.call-start
  8.0 0.7 all-gather.5.cloned.1.call-update
  8.7 0.0 copy-done.10
  8.7 0.2 reduce-window.8
  8.9 0.0 copy-done.2
  8.9 0.1 convert_reduce_fusion.1
  9.0 0.1 select_reduce_fusion
  9.1 0.0 copy-done
  9.1 0.1 convert_reduce_fusion
  9.2 0.3 fusion.23
  9.5 0.0 copy-start.6
  9.5 0.0 copy-done.1
  9.5 0.3 fusion.21
  9.9 93.2 %all-gather.7.cloned.1.call-done = bf16[1,1536,3072]{2,1,0:T(8,128)(2,1)} async-done(((bf16[1,192,3072]{2,1,0:T(8,128)(2,1)}), bf16[1,1536,3072]{2,1,0:T(8,128)(2,1)}) %all-gather.7.cloned.1.call-update) | async-done | bytes 9437200 | tf_op jit(solution)/shard_map/all_gather | solution.py:34
  103.1 90.9 %all-gather.5.cloned.1.call-done = bf16[1,3072,1536]{1,2,0:T(8,128)(2,1)} async-done(((bf16[1,3072,192]{1,2,0:T(8,128)(2,1)}), bf16[1,3072,1536]{1,2,0:T(8,128)(2,1)}) %all-gather.5.cloned.1.call-update) | async-done | bytes 9437200 | tf_op jit(solution)/shard_map/all_gather | solution.py:35
  194.0 0.0 copy-done.6
  194.0 0.6 conditional.4
  194.0 0.6 broadcast.129
  194.6 1.3 collective-permute-start
  195.9 11.9 %collective-permute-done = bf16[128,1536]{1,0:T(8,128)(2,1)S(1)} collective-permute-done((bf16[128,1536]{1,0:T(8,128)(2,1)S(1)}, bf16[128,1536]{1,0:T(8,128)(2,1)S(1)}, u32[]{:S(2)}, u32[]{:S(2)}) %collective-permute-start) | collective-permute-done | bytes 393248 | tf_op jit(solution)/shard_map/ppermute | solution.py:10
  207.8 0.0 copy-start.4
  207.8 1.3 collective-permute-start.1
  209.1 11.7 %collective-permute-done.1 = bf16[128,1536]{1,0:T(8,128)(2,1)S(1)} collective-permute-done((bf16[128,1536]{1,0:T(8,128)(2,1)S(1)}, bf16[128,1536]{1,0:T(8,128)(2,1)S(1)}, u32[]{:S(2)}, u32[]{:S(2)}) %collective-permute-start.1) | collective-permute-done | bytes 393248 | tf_op jit(solution)/shard_map/ppermute | solution.py:10
  220.8 0.0 copy-done.4
  220.8 0.6 conditional.6
  220.8 0.6 broadcast.137
  221.4 1.3 collective-permute-start.2
  222.7 66.6 %collective-permute-done.2 = bf16[128,1536]{1,0:T(8,128)(2,1)S(1)} collective-permute-done((bf16[128,1536]{1,0:T(8,128)(2,1)S(1)}, bf16[128,1536]{1,0:T(8,128)(2,1)S(1)}, u32[]{:S(2)}, u32[]{:S(2)}) %collective-permute-start.2) | collective-permute-done | bytes 393248 | tf_op jit(solution)/shard_map/ppermute | solution.py:10
  289.3 0.0 copy-start.3
  289.3 0.0 copy-start.5
  289.3 20.4 %conditional.7 = (bf16[128,1536]{1,0:T(8,128)(2,1)S(1)}, f32[1536]{0:T(1024)S(1)}) conditional(s32[]{:T(128)} %convert_element_type.77, bf16[128,1536]{1,0:T(8,128)(2,1)S(1)} %collective-permute-done.2, (bf16[128,1536]{1,0:T(8,128)(2,1)S(1)}, f32[128,1]{0,1:T(1,128)}, bf16[3072,1536]{0,1:T(8,128)(2,1)}, bf16[128,1536]{1,0:T(8,128)(2,1)S(1)}, ...), branch_computations={%region_20.21_spmd, %region_21.25_spmd} | conditional | flops 3630562048 | bytes 36213296 | solution.py:72
  289.3 6.2 %fusion.28 = f32[128,3072]{1,0:T(8,128)} fusion(bf16[128,1536]{1,0:T(8,128)(2,1)S(1)} %get-tuple-element.84, bf16[1536,3072]{1,0:T(8,128)(2,1)} %get-tuple-element.85), kind=kOutput, calls=%fused_computation.69 | convolution fusion | flops 1207959552 | bytes 11403264 | tf_op jit(solution)/shard_map/cond/branch_1_fun/dot_general | solution.py:39
  295.5 0.0 copy-start.9
  295.5 12.7 %multiply_reduce_fusion.9 = (f32[1536]{0:T(1024)S(1)}, f32[128]{0:T(128)S(1)}, f32[128]{0:T(128)S(1)}, f32[128,1536]{1,0:T(8,128)}) fusion(f32[128,1536]{1,0:T(8,128)S(1)} %get-tuple-element.87, f32[1536]{0:T(1024)S(1)} %reduce.4, bf16[1536,3072]{1,0:T(8,128)(2,1)} %get-tuple-element.85, bf16[128,1536]{1,0:T(8,128)(2,1)S(1)} %get-tuple-element.81, ...), kind=kOutput, calls=%fused_computation.39 | convolution fusion | flops 2421029376 | bytes 22426624 | tf_op jit(solution)/shard_map/cond/branch_1_fun/dot_general | solution.py:43
  308.2 0.0 copy-done.9
  308.2 1.4 add_convert_fusion.3
  309.7 0.0 copy-done.3
  309.7 0.0 copy-done.5
  309.7 0.8 select_bitcast_fusion
  310.6 14.5 %psum.7 = f32[1,1536]{1,0:T(1,128)} all-reduce(f32[1,1536]{1,0:T(1,128)S(1)} %broadcast_in_dim.5), channel_id=1, replica_groups=mesh['segment'=4,'dp'=8] {'dp'}, use_global_device_ids=true, to_apply=%region_25.26 | all-reduce | flops 1536 | bytes 12288 | tf_op jit(solution)/shard_map/psum | solution.py:77
  (12 shorter events, 0.1 us)
Async XLA Ops:
  7.2 1.5 copy-start.10
  7.2 1.7 copy-start.2
  7.2 1.9 copy-start
  7.2 2.3 copy-start.1
  7.2 95.9 %all-gather.7.cloned.1.call-start = ((), (), s32[]{:S(2)}) async-start(), calls=%async_computation.1 | async-start | bytes 10616832 | tf_op jit(solution)/shard_map/all_gather | solution.py:34
  7.9 186.1 %all-gather.5.cloned.1.call-start = ((), (), s32[]{:S(2)}) async-start(), calls=%async_computation | async-start | bytes 10616832 | tf_op jit(solution)/shard_map/all_gather | solution.py:35
  9.5 184.5 %copy-start.6 = (f32[128,1]{0,1:T(1,128)}, f32[128,1]{0,1:T(1,128)S(1)}, u32[]{:S(2)}) copy-start(f32[128,1]{0,1:T(1,128)S(1)} %get-tuple-element.189) | copy-start | bytes 1540
  194.6 13.2 %collective-permute-start = (bf16[128,1536]{1,0:T(8,128)(2,1)S(1)}, bf16[128,1536]{1,0:T(8,128)(2,1)S(1)}, u32[]{:S(2)}, u32[]{:S(2)}) collective-permute-start(bf16[128,1536]{1,0:T(8,128)(2,1)S(1)} %get-tuple-element.98), channel_id=1, source_target_pairs={{8,0},{16,8},{24,16},{9,1},{17,9},{25,17},{10,2},{18,10},{26,18},{... | collective-permute-start | bytes 1179656 | tf_op jit(solution)/shard_map/ppermute | solution.py:10
  207.8 13.0 %copy-start.4 = (f32[1536]{0:T(1024)}, f32[1536]{0:T(1024)S(1)}, u32[]{:S(2)}) copy-start(f32[1536]{0:T(1024)S(1)} %get-tuple-element.104) | copy-start | bytes 18436
  207.8 13.0 %collective-permute-start.1 = (bf16[128,1536]{1,0:T(8,128)(2,1)S(1)}, bf16[128,1536]{1,0:T(8,128)(2,1)S(1)}, u32[]{:S(2)}, u32[]{:S(2)}) collective-permute-start(bf16[128,1536]{1,0:T(8,128)(2,1)S(1)} %get-tuple-element.99), channel_id=1, source_target_pairs={{8,0},{16,8},{24,16},{9,1},{17,9},{25,17},{10,2},{18,10},{26,18},{... | collective-permute-start | bytes 1179656 | tf_op jit(solution)/shard_map/ppermute | solution.py:10
  221.4 67.9 %collective-permute-start.2 = (bf16[128,1536]{1,0:T(8,128)(2,1)S(1)}, bf16[128,1536]{1,0:T(8,128)(2,1)S(1)}, u32[]{:S(2)}, u32[]{:S(2)}) collective-permute-start(bf16[128,1536]{1,0:T(8,128)(2,1)S(1)} %get-tuple-element.100), channel_id=1, source_target_pairs={{8,0},{16,8},{24,16},{9,1},{17,9},{25,17},{10,2},{18,10},{26,18},{... | collective-permute-start | bytes 1179656 | tf_op jit(solution)/shard_map/ppermute | solution.py:10
  289.3 20.4 %copy-start.3 = (f32[1536]{0:T(1024)S(1)}, f32[1536]{0:T(1024)}, u32[]{:S(2)}) copy-start(f32[1536]{0:T(1024)} %get-tuple-element.105) | copy-start | bytes 18436
  289.3 20.4 %copy-start.5 = (f32[1536]{0:T(1024)S(1)}, f32[1536]{0:T(1024)}, u32[]{:S(2)}) copy-start(f32[1536]{0:T(1024)} %copy-done.4) | copy-start | bytes 18436
  295.5 12.7 %copy-start.9 = (f32[128,1]{0,1:T(1,128)S(1)}, f32[128,1]{0,1:T(1,128)}, u32[]{:S(2)}) copy-start(f32[128,1]{0,1:T(1,128)} %get-tuple-element.82) | copy-start | bytes 1540 | tf_op jit(solution)/shard_map/cond
Sparse Core Ops, SparseCore 0:
  9.7 93.4 all-gather.6
  104.8 89.1 all-gather.4
where the time goes:
time: 332 us
  waiting for transfers between devices  276 us (83%)
  matrix products  18.9 us (6%)
  blocking collectives  14.5 us (4%)
  between operations  14.2 us (4%)
  starting transfers between devices  3.92 us (1%)
  other arithmetic  3.44 us (1%)
    all_gather x1, waiting for transfers between devices, on_device(): lax.all_gather(w_in[0], 'dp', axis=0, tiled=True)  93.2 us
    all_gather x1, waiting for transfers between devices, on_device(): lax.all_gather(w_out[0], 'dp', axis=1, tiled=True)  90.9 us
    ppermute x3, waiting for transfers between devices, passed_along(): return lax.ppermute(x, axis, pairs)  90.2 us
    psum x1, blocking collectives, on_device(): gain_total = lax.psum(gain_local, 'dp')  14.5 us
    dot_general x1, matrix products, project_all(): return jnp.dot(hid_grad, w_first.T, preferred_element_type=jnp.float32)  12.7 us
  transfers between devices with their start and end apart: 5, of which 5 were waited for; matrix products, arithmetic and copies ran while one was open for 0% of the time, Pallas kernels for 0%

commit v1 on v0

--- a/solution.py
+++ b/solution.py
@@ -1,7 +1,15 @@
+import functools
+
 import jax
 import jax.numpy as jnp
 from jax import lax
+from jax.experimental import pallas as pl
+from jax.experimental.pallas import tpu as pltpu
 from jax.sharding import PartitionSpec as P
+
+MESH = pl.DeviceIdType.MESH
+PIECES = 6
+CHUNK = 128
 
 
 def passed_along(x, axis, by):
@@ -32,7 +40,7 @@
     normalized_input = (standardized_input * gain_vector).astype(jnp.bfloat16)
     w_first, w_second = (
         lax.all_gather(w_in[0], "dp", axis=0, tiled=True),
-        lax.all_gather(w_out[0], "dp", axis=1, tiled=True),
+        lax.all_gather(w_out[0].T, "dp", axis=0, tiled=True).T,
     )
 
     def project_all(normed_rows, grad_in):
@@ -42,23 +50,19 @@
         hid_grad = (0.5 * up_grad * (sig + hidden * sig * (1.0 - sig))).astype(jnp.bfloat16)
         return jnp.dot(hid_grad, w_first.T, preferred_element_type=jnp.float32)
 
-    def block_back():
-
-        def run(grad_in):
-            norm_gradient = project_all(normalized_input, grad_in)
-            gain_partial = jnp.sum(norm_gradient * standardized_input, 0)
-            gain_scaled = norm_gradient * gain_vector
-            backward_result = inverse_deviation * (
-                gain_scaled
-                - jnp.mean(gain_scaled, -1, keepdims=True)
-                - standardized_input * jnp.mean(gain_scaled * standardized_input, -1, keepdims=True)
-            )
-            return (
-                (grad_in.astype(jnp.float32) + backward_result).astype(jnp.bfloat16),
-                gain_partial,
-            )
-
-        return run
+    def block_back(grad_in):
+        norm_gradient = project_all(normalized_input, grad_in)
+        gain_partial = jnp.sum(norm_gradient * standardized_input, 0)
+        gain_scaled = norm_gradient * gain_vector
+        backward_result = inverse_deviation * (
+            gain_scaled
+            - jnp.mean(gain_scaled, -1, keepdims=True)
+            - standardized_input * jnp.mean(gain_scaled * standardized_input, -1, keepdims=True)
+        )
+        return (
+            (grad_in.astype(jnp.float32) + backward_result).astype(jnp.bfloat16),
+            gain_partial,
+        )
 
     def pass_through(grad_in):
         return (grad_in, jnp.zeros((width,), jnp.float32))
@@ -69,13 +73,346 @@
     result = current
     for level in range(segments - 1, -1, -1):
         mine = my_segment == level
-        updated, gain_partial = lax.cond(mine, block_back(), pass_through, current)
+        updated, gain_partial = lax.cond(mine, block_back, pass_through, current)
         result = jnp.where(mine, updated, result)
         gain_local = jnp.where(mine, gain_partial, gain_local)
         if level > 0:
             current = passed_along(updated, "segment", -1)
     gain_total = lax.psum(gain_local, "dp")
     return (result[None], gain_total[None])
+
+
+def kernel(
+    segments, utts,
+    x_ref, gain_ref, wst_ref, cot_ref, len_ref, out_ref, gg_ref,
+    W, F, dz, xh, zb, g, gn, inv, xin, slots,
+    lsem, hs, hr, os_, or_, fs, fr, ps, pr, xs, xr, ts, tr, gs, gr, rs, rr, qs, qr,
+):
+    D = x_ref.shape[1]
+    T = x_ref.shape[0]
+    depth = wst_ref.shape[1]
+    FF = wst_ref.shape[2]
+    blk = FF // PIECES
+    R2 = 2 * T
+    n_chunks = R2 // CHUNK
+
+    s = lax.axis_index("segment")
+    k = lax.axis_index("dp")
+    z = k // 2
+    c = k % 2
+    worker = (z == 1) | (z == 2)
+    helper = (z == 0) | (z == 3)
+    top_seg = s == segments - 1
+    zw = 1 + z // 2
+    zh = 3 * (z // 2)
+    zo = 3 - zw
+    zoh = 3 - zh
+    partner = 2 * z + (1 - c)
+    sources = (zw, zh, zo, zoh)
+
+    barrier = pltpu.get_barrier_semaphore()
+    for d in range(1, 8):
+        pl.semaphore_signal(
+            barrier, inc=1, device_id={"dp": lax.rem(k + d, 8)}, device_id_type=MESH
+        )
+
+    @pl.when(s > 0)
+    def _():
+        pl.semaphore_signal(barrier, inc=1, device_id={"segment": s - 1}, device_id_type=MESH)
+
+    @pl.when(s < segments - 1)
+    def _():
+        pl.semaphore_signal(barrier, inc=1, device_id={"segment": s + 1}, device_id_type=MESH)
+
+    near = (s > 0).astype(jnp.int32) + (s < segments - 1).astype(jnp.int32)
+    pl.semaphore_wait(barrier, 7 + near)
+
+    def rows_of(zz, cc):
+        return pl.ds(pl.multiple_of((2 * zz + cc) * depth, depth), depth)
+
+    def cols_of(p):
+        return pl.ds(pl.multiple_of(p * blk, blk), blk)
+
+    def remote(src, dst, ssem, rsem, dev):
+        return pltpu.make_async_remote_copy(
+            src_ref=src, dst_ref=dst, send_sem=ssem, recv_sem=rsem,
+            device_id=dev, device_id_type=MESH,
+        )
+
+    def own_src(p):
+        return wst_ref.at[:, :, cols_of(p)]
+
+    def slot(zz, cc, p):
+        return W.at[:, rows_of(zz, cc), cols_of(p)]
+
+    def to_worker(p):
+        return remote(own_src(p), slot(z, c, p), hs.at[p], hr.at[p], {"dp": 2 * zw + c})
+
+    def from_helper(p):
+        return remote(slot(zh, c, p), slot(zh, c, p), hs.at[p], hr.at[p], {"dp": 2 * zh + c})
+
+    def own_to_other(p):
+        return remote(own_src(p), slot(z, c, p), os_.at[p], or_.at[p], {"dp": 2 * zo + c})
+
+    def own_from_other(p):
+        return remote(own_src(p), slot(zo, c, p), os_.at[p], or_.at[p], {"dp": 2 * zo + c})
+
+    def fwd_to_other(p):
+        return remote(slot(zh, c, p), slot(zh, c, p), fs.at[p], fr.at[p], {"dp": 2 * zo + c})
+
+    def fwd_from_other(p):
+        return remote(slot(zoh, c, p), slot(zoh, c, p), fs.at[p], fr.at[p], {"dp": 2 * zo + c})
+
+    def to_partner(i, p):
+        src = own_src(p) if i == 0 else slot(sources[i], c, p)
+        return remote(src, slot(sources[i], c, p), ps.at[i, p], pr.at[i, p], {"dp": partner})
+
+    def from_partner(i, p):
+        there = slot(sources[i], 1 - c, p)
+        return remote(there, there, ps.at[i, p], pr.at[i, p], {"dp": partner})
+
+    local = pltpu.make_async_copy(wst_ref, W.at[:, rows_of(z, c), :], lsem)
+    top_rows = g.at[pl.ds(T, T), :]
+    x_send = remote(x_ref, xin.at[pl.ds(0, T), :], xs, xr, {"dp": 2 * zw + c})
+    x_recv = remote(x_ref, xin.at[pl.ds(0, T), :], xs, xr, {"dp": 2 * zh + c})
+    t_send = remote(top_rows, g.at[pl.ds(0, T), :], ts, tr, {"dp": 2 * zw + c})
+    t_recv = remote(top_rows, g.at[pl.ds(0, T), :], ts, tr, {"dp": 2 * zh + c})
+    ret_send = remote(gn.at[pl.ds(0, T), :], gn.at[pl.ds(T, T), :], rs, rr, {"dp": 2 * zh + c})
+    ret_recv = remote(gn.at[pl.ds(0, T), :], gn.at[pl.ds(T, T), :], rs, rr, {"dp": 2 * zw + c})
+
+    @pl.when(helper)
+    def _():
+        x_send.start()
+
+    @pl.when(worker)
+    def _():
+        own_to_other(0).start()
+        to_partner(0, 0).start()
+        local.start()
+
+    @pl.when(top_seg)
+    def _():
+        pos = k * T + lax.broadcasted_iota(jnp.int32, (T, 128), 0)
+        tok = jnp.zeros((T, 128), jnp.float32)
+        start = jnp.int32(0)
+        for j in range(utts):
+            n = len_ref[j]
+            hit = (pos >= start) & (pos < start + n)
+            tok = jnp.where(hit, n.astype(jnp.float32), tok)
+            start = start + n
+        weight = (2.0 * T / (tok + T))[:, 0:1]
+        g[T:, :] = (cot_ref[...].astype(jnp.float32) * weight).astype(jnp.bfloat16)
+
+    @pl.when(helper & top_seg)
+    def _():
+        t_send.start()
+
+    @pl.when(helper)
+    def _():
+        @pl.loop(0, PIECES)
+        def _(p):
+            to_worker(p).start()
+
+    NORM = 64
+
+    @pl.when(worker)
+    def _():
+        xin[T:, :] = x_ref[...]
+        x_recv.wait_recv()
+
+        @pl.loop(0, R2 // NORM)
+        def _(i):
+            r = pl.ds(pl.multiple_of(i * NORM, NORM), NORM)
+            xf = xin[r, :].astype(jnp.float32)
+            cen = xf - jnp.mean(xf, -1, keepdims=True)
+            iv = lax.rsqrt(jnp.mean(cen * cen, -1, keepdims=True) + 1e-05)
+            xhat = cen * iv
+            inv[r, :] = jnp.broadcast_to(iv, (NORM, 128))
+            xh[r, :] = xhat
+            zb[r, :] = (xhat * gain_ref[...]).astype(jnp.bfloat16)
+            dz[r, :] = jnp.zeros((NORM, D), jnp.float32)
+
+        @pl.when(top_seg)
+        def _():
+            t_recv.wait_recv()
+
+        local.wait()
+
+    def hidden(p):
+        h = jnp.dot(zb[...], W[0, :, cols_of(p)], preferred_element_type=jnp.float32)
+        sig = jax.nn.sigmoid(h)
+        F[:, cols_of(p)] = 0.5 * (sig + h * sig * (1.0 - sig))
+
+    def back(p, r):
+        u = jnp.dot(g[r, :], W[1, :, cols_of(p)], preferred_element_type=jnp.float32)
+        du = (u * F[r, cols_of(p)]).astype(jnp.bfloat16)
+        dz[r, :] += lax.dot_general(
+            du, W[0, :, cols_of(p)], (((1,), (1,)), ((), ())),
+            preferred_element_type=jnp.float32,
+        )
+
+    @pl.when(worker)
+    def _():
+        @pl.loop(0, PIECES)
+        def _(p):
+            @pl.when(p + 1 < PIECES)
+            def _():
+                own_to_other(p + 1).start()
+                to_partner(0, p + 1).start()
+
+            from_helper(p).wait_recv()
+            fwd_to_other(p).start()
+            to_partner(1, p).start()
+            own_from_other(p).wait_recv()
+            to_partner(2, p).start()
+            fwd_from_other(p).wait_recv()
+            to_partner(3, p).start()
+            for i in range(4):
+                from_partner(i, p).wait_recv()
+            hidden(p)
+
+            @pl.when(top_seg)
+            def _():
+                back(p, pl.ds(0, R2))
+
+    def g_copy(i, to):
+        r = pl.ds(pl.multiple_of(i * CHUNK, CHUNK), CHUNK)
+        return remote(gn.at[r, :], g.at[r, :], gs.at[i], gr.at[i], {"segment": to})
+
+    wi = jnp.clip((z - 1) * 2 + c, 0, 3)
+    EP = 64
+
+    @pl.when(worker)
+    def _():
+        slots[wi] = jnp.zeros((1, D), jnp.float32)
+
+        @pl.loop(0, n_chunks)
+        def _(i):
+            r = pl.ds(pl.multiple_of(i * CHUNK, CHUNK), CHUNK)
+
+            @pl.when(jnp.logical_not(top_seg))
+            def _():
+                g_copy(i, s + 1).wait_recv()
+
+                @pl.loop(0, PIECES)
+                def _(p):
+                    back(p, r)
+
+            @pl.loop(0, CHUNK // EP)
+            def _(j):
+                q = pl.ds(pl.multiple_of(i * CHUNK + j * EP, EP), EP)
+                d = dz[q, :]
+                xhat = xh[q, :]
+                t = d * xhat
+                slots[wi] += jnp.sum(t, 0, keepdims=True)
+                gain = gain_ref[...]
+                e = d * gain
+                m1 = jnp.mean(e, -1, keepdims=True)
+                m2 = jnp.mean(t * gain, -1, keepdims=True)
+                gn[q, :] = (
+                    g[q, :].astype(jnp.float32) + inv[q, 0:1] * (e - m1 - xhat * m2)
+                ).astype(jnp.bfloat16)
+
+            @pl.when(s > 0)
+            def _():
+                g_copy(i, s - 1).start()
+
+            @pl.when((i + 1) * CHUNK == T)
+            def _():
+                ret_send.start()
+
+    def q_copy(d):
+        return remote(slots.at[wi], slots.at[wi], qs.at[d], qr.at[wi], {"dp": lax.rem(k + d, 8)})
+
+    @pl.when(worker)
+    def _():
+        for d in range(1, 8):
+            q_copy(d).start()
+        out_ref[...] = gn[T:, :]
+
+    @pl.when(helper)
+    def _():
+        ret_recv.wait_recv()
+        out_ref[...] = gn[T:, :]
+
+    for w in range(4):
+        @pl.when(k != w + 2)
+        def _(w=w):
+            remote(
+                slots.at[w], slots.at[w], qs.at[0], qr.at[w], {"dp": partner}
+            ).wait_recv()
+
+    gg_ref[...] = slots[0] + slots[1] + slots[2] + slots[3]
+
+    @pl.when(worker)
+    def _():
+        for d in range(1, 8):
+            q_copy(d).wait_send()
+        ret_send.wait_send()
+
+        @pl.loop(0, PIECES)
+        def _(p):
+            own_to_other(p).wait_send()
+            fwd_to_other(p).wait_send()
+            for i in range(4):
+                to_partner(i, p).wait_send()
+
+        @pl.when(s > 0)
+        def _():
+            @pl.loop(0, n_chunks)
+            def _(i):
+                g_copy(i, s - 1).wait_send()
+
+    @pl.when(helper)
+    def _():
+        x_send.wait_send()
+
+        @pl.loop(0, PIECES)
+        def _(p):
+            to_worker(p).wait_send()
+
+        @pl.when(top_seg)
+        def _():
+            t_send.wait_send()
+
+
+def in_kernel(segments, x_saved, gains, w_in, w_out, cotangent, lengths):
+    T, D = cotangent.shape
+    FF = w_in.shape[2]
+    wst = jnp.stack([w_in[0], w_out[0].T])
+    R2 = 2 * T
+    DMA = pltpu.SemaphoreType.DMA
+    bf, f32 = jnp.bfloat16, jnp.float32
+    vmem = pl.BlockSpec(memory_space=pltpu.VMEM)
+    grads, gg = pl.pallas_call(
+        functools.partial(kernel, segments, lengths.shape[0]),
+        out_shape=(jax.ShapeDtypeStruct((T, D), bf), jax.ShapeDtypeStruct((1, D), f32)),
+        in_specs=[
+            vmem, vmem, pl.BlockSpec(memory_space=pl.ANY), vmem,
+            pl.BlockSpec(memory_space=pltpu.SMEM),
+        ],
+        out_specs=(vmem, vmem),
+        scratch_shapes=[
+            pltpu.VMEM((2, D, FF), bf),
+            pltpu.VMEM((R2, FF), f32),
+            pltpu.VMEM((R2, D), f32),
+            pltpu.VMEM((R2, D), f32),
+            pltpu.VMEM((R2, D), bf),
+            pltpu.VMEM((R2, D), bf),
+            pltpu.VMEM((R2, D), bf),
+            pltpu.VMEM((R2, 128), f32),
+            pltpu.VMEM((R2, D), bf),
+            pltpu.VMEM((4, 1, D), f32),
+            DMA, DMA((PIECES,)), DMA((PIECES,)), DMA((PIECES,)), DMA((PIECES,)),
+            DMA((PIECES,)), DMA((PIECES,)), DMA((4, PIECES)), DMA((4, PIECES)),
+            DMA, DMA, DMA, DMA, DMA((R2 // CHUNK,)), DMA((R2 // CHUNK,)),
+            DMA, DMA, DMA((8,)), DMA((4,)),
+        ],
+        compiler_params=pltpu.CompilerParams(
+            collective_id=0, has_side_effects=True, vmem_limit_bytes=56 * 1024 * 1024
+        ),
+    )(x_saved[0], gains, wst, cotangent, lengths)
+    return (grads[None], gg)
 
 
 def solution(mesh):
@@ -88,6 +425,9 @@
         P(),
     )
     out_specs = (P("segment", "dp", None), P("segment", None))
+    body = on_device
+    if mesh.shape["dp"] == 8:
+        body = functools.partial(in_kernel, mesh.shape["segment"])
     return jax.shard_map(
-        on_device, mesh=mesh, in_specs=in_specs, out_specs=out_specs, check_vma=False
+        body, mesh=mesh, in_specs=in_specs, out_specs=out_specs, check_vma=False
     )

time: 332 us -> 214 us (0.64)
  waiting for transfers between devices: 276 us -> 0 us
  Pallas kernels: 0 us -> 207 us
  matrix products: 18.9 us -> 0 us
  blocking collectives: 14.5 us -> 0 us
  between operations: 14.2 us -> 0.64 us
  starting transfers between devices: 3.92 us -> 0 us
    pallas_call x0 -> x1, Pallas kernels: none -> 207 us  [in_kernel(): pl.pallas_call(functools.partial(kernel, segments, lengths.shape[0]), out...]
    all_gather x2 -> x0, waiting for transfers between devices: 184 us -> none  [the longest x1 93.2 us: on_device(): lax.all_gather(w_in[0], 'dp', axis=0, tiled=True)]
    ppermute x3 -> x0, waiting for transfers between devices: 90.2 us -> none  [passed_along(): return lax.ppermute(x, axis, pairs)]
    dot_general x2 -> x0, matrix products: 18.9 us -> none  [the longest x1 12.7 us: project_all(): return jnp.dot(hid_grad, w_first.T, preferred_element_type=jnp.float32)]
    psum x1 -> x0, blocking collectives: 14.5 us -> none  [on_device(): gain_total = lax.psum(gain_local, 'dp')]
    ppermute x3 -> x0, starting transfers between devices: 3.84 us -> none  [passed_along(): return lax.ppermute(x, axis, pairs)]
  transfers between devices with their start and end apart: 5 -> 0, of which waited for: 5 -> 0; matrix products, arithmetic and copies ran while one was open for 0% -> 0% of each run, Pallas kernels for 0% -> 0%
where the time goes in v1:
time: 214 us
  Pallas kernels  207 us (97%)
  other arithmetic  3.25 us (2%)
  local copies, waits for them, and re-layouts  3.05 us (1%)
    pallas_call x1, Pallas kernels, in_kernel(): pl.pallas_call(functools.partial(kernel, segments, lengths.shape[0]), out...  207 us

profile of v1, /device:TPU:0, one launch (start us, length us, event | category | flops | bytes accessed | tf_op | source)
XLA Modules:
  0.0 214.1 jit_solution(14190027343232455251)
XLA Ops:
  0.6 3.3 %pad_maximum_fusion.wst_ref = bf16[2,192,3072]{2,1,0:T(8,128)(2,1)} fusion(bf16[1,192,3072]{2,1,0:T(8,128)(2,1)} %bitcast.7, bf16[1,192,3072]{2,1,0:T(8,128)(2,1)} %param.8), kind=kLoop, calls=%fused_computation | loop fusion | flops 1179648 | bytes 4718592 | tf_op jit(solution)/shard_map/stack | solution.py:382
  3.9 207.2 %shard_map.77 = (bf16[128,1536]{1,0:T(8,128)(2,1)}, f32[1,1536]{1,0:T(1,128)}) custom-call(bf16[128,1536]{1,0:T(8,128)(2,1)} %bitcast.8, f32[1,1536]{1,0:T(1,128)} %gain_ref.1, bf16[2,192,3072]{2,1,0:T(8,128)(2,1)} %pad_maximum_fusion.wst_ref, bf16[128,1536]{1,0:T(8,128)(2,1)} %cot_ref.1, s32[8]{0:T(128)} %len_ref.1), custom_call_target="tpu_custom_call" | custom-call | tf_op jit(solution)/shard_map/pallas_call | solution.py:387
  211.1 1.8 copy.10
  212.9 1.3 copy.11

commit v2 on v1

--- a/solution.py
+++ b/solution.py
@@ -8,8 +8,8 @@
 from jax.sharding import PartitionSpec as P
 
 MESH = pl.DeviceIdType.MESH
-PIECES = 6
-CHUNK = 128
+PIECES = 4
+CHUNK = 64
 
 
 def passed_along(x, axis, by):
@@ -21,7 +21,8 @@
 def on_device(x_saved, gains, w_in, w_out, cotangent, lengths):
     rows = cotangent.shape[0]
     width = cotangent.shape[1]
-    ends = jnp.cumsum(lengths)
+    index = jnp.arange(lengths.shape[0], dtype=jnp.int32)
+    ends = jnp.sum(jnp.where(index[:, None] <= index[None, :], lengths[:, None], 0), 0)
     position = lax.axis_index("dp") * rows + jnp.arange(rows, dtype=jnp.int32)
     utter_hit = (position[:, None] >= ends[None, :]).astype(jnp.int32)
     utter = jnp.sum(utter_hit, 1)
@@ -90,8 +91,8 @@
 ):
     D = x_ref.shape[1]
     T = x_ref.shape[0]
-    depth = wst_ref.shape[1]
-    FF = wst_ref.shape[2]
+    depth = wst_ref.shape[2]
+    FF = F.shape[1]
     blk = FF // PIECES
     R2 = 2 * T
     n_chunks = R2 // CHUNK
@@ -140,10 +141,10 @@
         )
 
     def own_src(p):
-        return wst_ref.at[:, :, cols_of(p)]
+        return wst_ref.at[p]
 
     def slot(zz, cc, p):
-        return W.at[:, rows_of(zz, cc), cols_of(p)]
+        return W.at[p, :, rows_of(zz, cc), :]
 
     def to_worker(p):
         return remote(own_src(p), slot(z, c, p), hs.at[p], hr.at[p], {"dp": 2 * zw + c})
@@ -171,7 +172,7 @@
         there = slot(sources[i], 1 - c, p)
         return remote(there, there, ps.at[i, p], pr.at[i, p], {"dp": partner})
 
-    local = pltpu.make_async_copy(wst_ref, W.at[:, rows_of(z, c), :], lsem)
+    local = pltpu.make_async_copy(wst_ref, W.at[:, :, rows_of(z, c), :], lsem)
     top_rows = g.at[pl.ds(T, T), :]
     x_send = remote(x_ref, xin.at[pl.ds(0, T), :], xs, xr, {"dp": 2 * zw + c})
     x_recv = remote(x_ref, xin.at[pl.ds(0, T), :], xs, xr, {"dp": 2 * zh + c})
@@ -188,6 +189,8 @@
     def _():
         own_to_other(0).start()
         to_partner(0, 0).start()
+        own_to_other(1).start()
+        to_partner(0, 1).start()
         local.start()
 
     @pl.when(top_seg)
@@ -239,26 +242,35 @@
         local.wait()
 
     def hidden(p):
-        h = jnp.dot(zb[...], W[0, :, cols_of(p)], preferred_element_type=jnp.float32)
+        h = jnp.dot(zb[...], W[p, 0], preferred_element_type=jnp.float32)
         sig = jax.nn.sigmoid(h)
         F[:, cols_of(p)] = 0.5 * (sig + h * sig * (1.0 - sig))
 
     def back(p, r):
-        u = jnp.dot(g[r, :], W[1, :, cols_of(p)], preferred_element_type=jnp.float32)
+        u = jnp.dot(g[r, :], W[p, 1], preferred_element_type=jnp.float32)
         du = (u * F[r, cols_of(p)]).astype(jnp.bfloat16)
         dz[r, :] += lax.dot_general(
-            du, W[0, :, cols_of(p)], (((1,), (1,)), ((), ())),
+            du, W[p, 0], (((1,), (1,)), ((), ())),
             preferred_element_type=jnp.float32,
         )
 
+    def piece(p):
+        for i in range(4):
+            from_partner(i, p).wait_recv()
+        hidden(p)
+
+        @pl.when(top_seg)
+        def _():
+            back(p, pl.ds(0, R2))
+
     @pl.when(worker)
     def _():
         @pl.loop(0, PIECES)
         def _(p):
-            @pl.when(p + 1 < PIECES)
+            @pl.when(p + 2 < PIECES)
             def _():
-                own_to_other(p + 1).start()
-                to_partner(0, p + 1).start()
+                own_to_other(p + 2).start()
+                to_partner(0, p + 2).start()
 
             from_helper(p).wait_recv()
             fwd_to_other(p).start()
@@ -267,13 +279,11 @@
             to_partner(2, p).start()
             fwd_from_other(p).wait_recv()
             to_partner(3, p).start()
-            for i in range(4):
-                from_partner(i, p).wait_recv()
-            hidden(p)
-
-            @pl.when(top_seg)
+            @pl.when(p > 0)
             def _():
-                back(p, pl.ds(0, R2))
+                piece(p - 1)
+
+        piece(PIECES - 1)
 
     def g_copy(i, to):
         r = pl.ds(pl.multiple_of(i * CHUNK, CHUNK), CHUNK)
@@ -379,7 +389,13 @@
 def in_kernel(segments, x_saved, gains, w_in, w_out, cotangent, lengths):
     T, D = cotangent.shape
     FF = w_in.shape[2]
-    wst = jnp.stack([w_in[0], w_out[0].T])
+    wst = jnp.stack(
+        [
+            w_in[0].reshape(-1, PIECES, FF // PIECES).transpose(1, 0, 2),
+            w_out[0].reshape(PIECES, FF // PIECES, -1).transpose(0, 2, 1),
+        ],
+        1,
+    )
     R2 = 2 * T
     DMA = pltpu.SemaphoreType.DMA
     bf, f32 = jnp.bfloat16, jnp.float32
@@ -393,7 +409,7 @@
         ],
         out_specs=(vmem, vmem),
         scratch_shapes=[
-            pltpu.VMEM((2, D, FF), bf),
+            pltpu.VMEM((PIECES, 2, D, FF // PIECES), bf),
             pltpu.VMEM((R2, FF), f32),
             pltpu.VMEM((R2, D), f32),
             pltpu.VMEM((R2, D), f32),

time: 214 us -> 187 us (0.87)
  Pallas kernels: 207 us -> 176 us
  local copies, waits for them, and re-layouts: 3.05 us -> 8.04 us
    pallas_call x1, Pallas kernels: 207 us -> 176 us  [in_kernel(): pl.pallas_call(functools.partial(kernel, segments, lengths.shape[0]), out...]
    another operation x0 -> x4, local copies, waits for them, and re-layouts: none -> 3.85 us  [the longest x2 2.83 us: in_kernel(): w_in[0].reshape(-1, PIECES, FF // PIECES).transpose(1, 0, 2)]
where the time goes in v2:
time: 187 us
  Pallas kernels  176 us (94%)
  local copies, waits for them, and re-layouts  8.04 us (4%)
    pallas_call x1, Pallas kernels, in_kernel(): pl.pallas_call(functools.partial(kernel, segments, lengths.shape[0]), out...  176 us
    unnamed x4, local copies, waits for them, and re-layouts  4.19 us

profile of v2, /device:TPU:0, one launch (start us, length us, event | category | flops | bytes accessed | tf_op | source)
XLA Modules:
  0.0 186.6 jit_solution(22622720323160428)
XLA Ops:
  0.6 2.7 %reshape_squeeze.6 = bf16[192,4,768]{2,1,0:T(4,128)(2,1)S(1)} reshape(bf16[1,192,3072]{2,1,0:T(8,128)(2,1)} %param.8) | data formatting | bytes 2359296 | tf_op jit(solution)/shard_map/reshape;squeeze | solution.py:394
  3.3 0.0 copy-start
  3.4 0.1 copy.13
  3.5 1.1 copy-done
  4.6 0.9 reshape_squeeze.7
  5.5 0.1 copy.12
  5.7 1.6 pad_maximum_fusion.wst_ref
  7.3 176.2 %shard_map.77 = (bf16[128,1536]{1,0:T(8,128)(2,1)}, f32[1,1536]{1,0:T(1,128)}) custom-call(bf16[128,1536]{1,0:T(8,128)(2,1)} %bitcast.16, f32[1,1536]{1,0:T(1,128)} %gain_ref.1, bf16[4,2,192,768]{3,2,1,0:T(8,128)(2,1)} %pad_maximum_fusion.wst_ref, bf16[128,1536]{1,0:T(8,128)(2,1)} %cot_ref.1, s32[8]{0:T(128)} %len_ref.1), custom_call_target="tpu_custom_call" | custom-call | tf_op jit(solution)/shard_map/pallas_call | solution.py:403
  183.6 1.8 copy.16
  185.3 1.3 copy.17
Async XLA Ops:
  3.3 1.3 copy-start

commit v3 on v2

--- a/solution.py
+++ b/solution.py
@@ -8,7 +8,7 @@
 from jax.sharding import PartitionSpec as P
 
 MESH = pl.DeviceIdType.MESH
-PIECES = 4
+PIECES = 2
 CHUNK = 64
 
 

time: 187 us -> 185 us (0.989)
  Pallas kernels: 176 us -> 174 us
    pallas_call x1, Pallas kernels: 176 us -> 174 us  [in_kernel(): pl.pallas_call(functools.partial(kernel, segments, lengths.shape[0]), out...]
where the time goes in v3:
time: 185 us; the launch traced here: 184 us
  Pallas kernels  174 us (94%)
  local copies, waits for them, and re-layouts  8.64 us (5%)
    pallas_call x1, Pallas kernels, in_kernel(): pl.pallas_call(functools.partial(kernel, segments, lengths.shape[0]), out...  174 us
    unnamed x4, local copies, waits for them, and re-layouts  4.19 us

profile of v3, /device:TPU:0, one launch (start us, length us, event | category | flops | bytes accessed | tf_op | source)
XLA Modules:
  0.0 184.5 jit_solution(2991376575387980834)
XLA Ops:
  0.6 3.3 %reshape_squeeze.6 = bf16[192,2,1536]{2,1,0:T(2,128)(2,1)S(1)} reshape(bf16[1,192,3072]{2,1,0:T(8,128)(2,1)} %param.8) | data formatting | bytes 2359296 | tf_op jit(solution)/shard_map/reshape;squeeze | solution.py:394
  4.0 0.0 copy-start
  4.0 0.1 copy.13
  4.1 1.1 copy-done
  5.2 0.9 reshape_squeeze.7
  6.1 0.1 copy.12
  6.3 1.6 pad_maximum_fusion.wst_ref
  7.9 173.5 %shard_map.77 = (bf16[128,1536]{1,0:T(8,128)(2,1)}, f32[1,1536]{1,0:T(1,128)}) custom-call(bf16[128,1536]{1,0:T(8,128)(2,1)} %bitcast.16, f32[1,1536]{1,0:T(1,128)} %gain_ref.1, bf16[2,2,192,1536]{3,2,1,0:T(8,128)(2,1)} %pad_maximum_fusion.wst_ref, bf16[128,1536]{1,0:T(8,128)(2,1)} %cot_ref.1, s32[8]{0:T(128)} %len_ref.1), custom_call_target="tpu_custom_call" | custom-call | tf_op jit(solution)/shard_map/pallas_call | solution.py:403
  181.4 1.8 copy.16
  183.2 1.3 copy.17
Async XLA Ops:
  4.0 1.3 copy-start
